TPU v7x, 512 devices: a whole 4x8x8 slice. The times are simulated.
512 devices in a mesh: ctx: 64 (over y_lo, z, x), tp: 8 (over y_hi, core).
Axes of the slice: x: 4, y: 8 (y_hi: 4, y_lo: 2; y = y_hi * 2 + y_lo), z: 8, core: 2. Of those that a mesh axis runs over, the one named last changes fastest.
Arguments:
- queries: bfloat16 [16384, 8192], P('ctx', 'tp'), may hold values from -128 to 128
- cotangent: bfloat16 [16384, 8192], P('ctx', 'tp'), may hold values from -96 to 96
- image_keys: bfloat16 [64, 64, 1024], P('ctx', None, 'tp'), may hold values from -8 to 8
- image_values: bfloat16 [64, 64, 1024], P('ctx', None, 'tp'), may hold values from -6 to 6
- attn_gate: float32 [1], replicated, may hold values from 0.4 to 1.5
- block_mask: int32 [128, 64], P('ctx'), may hold values from 0 to 1, as said below
- image_owner: int32 [64], replicated, may hold values from 0 to 63, each once
Outputs:
- query_grad: bfloat16 [16384, 8192], P('ctx', 'tp')
- key_grad: bfloat16 [64, 64, 1024], P('ctx', None, 'tp')
- value_grad: bfloat16 [64, 64, 1024], P('ctx', None, 'tp')
- gate_grad: float32 [1], replicated
Inputs may be any that keep to these rules, and one draw needn't show every extreme that they name: `block_mask`: every text block reads at least one image; the 2 blocks of one index of ctx together read exactly 32 distinct images.
All inputs are finite; a program needn't handle non-finite values.
Results may differ from a plain program's by a relative error of at most 0.02.
Values may be sent and summed in bfloat16 or wider, within the bound.
A program may use at most 64 MiB of HBM per device.

v0:
```python
import math
import jax
import jax.numpy as jnp
from jax import lax
from jax.sharding import PartitionSpec as P

HD = 128
BLK = 128


def per_device(queries, cotangent, image_keys, image_values, attn_gate, block_mask, image_owner):
    tok_dev = queries.shape[0]
    local_kv = image_keys.shape[2] // HD
    local_heads = queries.shape[1] // HD
    groups = local_heads // local_kv
    img_tok = image_keys.shape[1]
    inv_root = 1.0 / math.sqrt(HD)
    read_most = lax.axis_size("ctx") // 2
    gathered_keys, gathered_values = (
        lax.all_gather(image_keys, "ctx", axis=0, tiled=True),
        lax.all_gather(image_values, "ctx", axis=0, tiled=True),
    )
    n_images = gathered_keys.shape[0]
    read_any = jnp.max(block_mask, axis=0)
    ranking = read_any * (2 * n_images) + (n_images - 1 - jnp.arange(n_images, dtype=jnp.int32))
    top_vals, image_ids = lax.top_k(ranking, read_most)
    is_read = read_any[image_ids] > 0
    slot_ids = image_owner[image_ids]
    block_keep = (block_mask[:, image_ids] > 0) & is_read[None, :]
    keep_mask = jnp.repeat(jnp.repeat(block_keep, BLK, axis=0), img_tok, axis=1)
    key_rows = jnp.take(gathered_keys, slot_ids, axis=0).reshape(read_most * img_tok, local_kv, HD)
    value_rows = jnp.take(gathered_values, slot_ids, axis=0).reshape(
        read_most * img_tok, local_kv, HD
    )
    query_heads = queries.reshape(tok_dev, local_kv, groups, HD).transpose(2, 0, 1, 3)
    cot_heads = cotangent.reshape(tok_dev, local_kv, groups, HD).transpose(2, 0, 1, 3)
    gate_value = jnp.tanh(attn_gate[0])

    def head_step(state_in, head_inputs):
        key_acc, value_acc, gate_acc = state_in
        query_one, cot_one = head_inputs
        scores = (
            jnp.einsum("tkd,skd->kts", query_one, key_rows, preferred_element_type=jnp.float32)
            * inv_root
        )
        scores = jnp.where(keep_mask, scores, -1e30)
        row_max = jnp.max(scores, axis=-1, keepdims=True)
        exp_terms = jnp.where(keep_mask, jnp.exp(scores - row_max), 0.0)
        prob_full = exp_terms / jnp.sum(exp_terms, axis=-1, keepdims=True)
        prob_half = prob_full.astype(jnp.bfloat16)
        attended = jnp.einsum(
            "kts,skd->tkd", prob_half, value_rows, preferred_element_type=jnp.float32
        )
        cot_f = cot_one.astype(jnp.float32)
        gate_part = jnp.sum(cot_f * attended)
        attn_grad = (gate_value * cot_f).astype(jnp.bfloat16)
        prob_grad = jnp.einsum(
            "tkd,skd->kts", attn_grad, value_rows, preferred_element_type=jnp.float32
        )
        row_delta = jnp.sum(attn_grad.astype(jnp.float32) * attended, axis=-1).T
        score_grad = (prob_full * (prob_grad - row_delta[:, :, None]) * inv_root).astype(
            jnp.bfloat16
        )
        query_grad = jnp.einsum(
            "kts,skd->tkd", score_grad, key_rows, preferred_element_type=jnp.float32
        ).astype(jnp.bfloat16)
        key_acc = key_acc + jnp.einsum(
            "kts,tkd->skd", score_grad, query_one, preferred_element_type=jnp.float32
        )
        value_acc = value_acc + jnp.einsum(
            "kts,tkd->skd", prob_half, attn_grad, preferred_element_type=jnp.float32
        )
        return ((key_acc, value_acc, gate_acc + gate_part), query_grad)

    zero_grads = jnp.zeros((read_most * img_tok, local_kv, HD), jnp.float32)
    init_state = (zero_grads, zero_grads, jnp.zeros((), jnp.float32))
    (key_acc, value_acc, gate_acc), head_grads = lax.scan(
        head_step, init_state, (query_heads, cot_heads)
    )
    query_grad = head_grads.transpose(1, 2, 0, 3).reshape(tok_dev, local_heads * HD)
    stacked = jnp.concatenate(
        [
            key_acc.reshape(read_most, img_tok, local_kv * HD),
            value_acc.reshape(read_most, img_tok, local_kv * HD),
        ],
        axis=-1,
    )
    stacked = jnp.where(is_read[:, None, None], stacked, 0.0)
    buffer = (
        jnp.zeros((n_images, img_tok, 2 * local_kv * HD), jnp.float32).at[slot_ids].add(stacked)
    )
    received = lax.all_to_all(buffer, "ctx", split_axis=0, concat_axis=0, tiled=True)
    summed = jnp.sum(received, axis=0, keepdims=True)
    key_grad = summed[:, :, : local_kv * HD].astype(jnp.bfloat16)
    value_grad = summed[:, :, local_kv * HD :].astype(jnp.bfloat16)
    gate_total = lax.psum(gate_acc, ("ctx", "tp"))
    term_count = tok_dev * lax.axis_size("ctx") * local_heads * lax.axis_size("tp") * HD
    gate_grad = ((1.0 - gate_value * gate_value) * gate_total / math.sqrt(term_count)).reshape(1)
    return (query_grad, key_grad, value_grad, gate_grad)


def solution(mesh):
    in_specs = (
        P("ctx", "tp"),
        P("ctx", "tp"),
        P("ctx", None, "tp"),
        P("ctx", None, "tp"),
        P(),
        P("ctx", None),
        P(),
    )
    out_specs = (P("ctx", "tp"), P("ctx", None, "tp"), P("ctx", None, "tp"), P())
    return jax.shard_map(
        per_device, mesh=mesh, in_specs=in_specs, out_specs=out_specs, check_vma=False
    )
```

profile of v0, /device:TPU:1, one launch (start us, length us, event | category | flops | bytes accessed | tf_op | source)
XLA Modules:
  0.0 885.6 jit_solution(12151461978923027463)
XLA Ops:
  10.9 2.0 top_k.11
  17.4 253.3 %all-gather.5.cloned.1.call-done = bf16[64,64,128]{2,1,0:T(8,128)(2,1)} async-done(((bf16[1,64,128]{2,1,0:T(8,128)(2,1)}), bf16[64,64,128]{2,1,0:T(8,128)(2,1)}) %all-gather.5.cloned.1.call-update) | async-done | bytes 1048592 | tf_op jit(solution)/shard_map/all_gather | solution.py:21
  270.7 1.9 gather_fusion.4
  272.6 297.7 %all-gather.3.cloned.1.call-done = bf16[64,64,128]{2,1,0:T(8,128)(2,1)} async-done(((bf16[1,64,128]{2,1,0:T(8,128)(2,1)}), bf16[64,64,128]{2,1,0:T(8,128)(2,1)}) %all-gather.3.cloned.1.call-update) | async-done | bytes 1048592 | tf_op jit(solution)/shard_map/all_gather | solution.py:20
  570.4 1.9 gather_fusion.3
  572.4 92.9 %while.17 = (s32[]{:T(128)}, f32[2048,1,128]{0,2,1:T(8,128)}, f32[2048,1,128]{0,2,1:T(8,128)}, f32[]{:T(128)}, bf16[8,256,1,128]{3,1,2,0:T(8,128)(2,1)}, /*index...) while((s32[]{:T(128)}, f32[2048,1,128]{0,2,1:T(8,128)}, ...), condition=%wide.region_7.9_spmd.clone, body=%wide.region_2.8_spmd.clone.sunk | while | flops 814710016 | bytes 48644448 | solution.py:77
  575.2 1.9 fusion.68
  577.8 1.4 fusion.69
  586.8 1.9 fusion.68
  589.4 1.4 fusion.69
  590.9 1.4 fusion.71
  598.4 1.9 fusion.68
  601.0 1.4 fusion.69
  602.5 1.4 fusion.71
  610.1 1.9 fusion.68
  612.7 1.4 fusion.69
  614.1 1.4 fusion.71
  621.7 1.9 fusion.68
  624.3 1.4 fusion.69
  633.3 1.9 fusion.68
  635.9 1.4 fusion.69
  644.9 1.9 fusion.68
  647.5 1.4 fusion.69
  656.5 1.9 fusion.68
  659.1 1.4 fusion.69
  665.3 1.6 copy.40
  668.3 1.4 maximum_select_fusion
  669.8 2.5 broadcast_in_dim.68
  672.2 6.4 scatter_fusion
  678.6 7.4 all-to-all-start
  686.0 186.7 %psum.7 = f32[]{:T(128)} all-reduce(f32[]{:T(128)} %get-tuple-element.72), channel_id=1, replica_groups=mesh['ctx'=64,'tp'=8] {'ctx','tp'}, use_global_device_ids=true, to_apply=%region_10.12 | all-reduce | flops 1 | bytes 8 | tf_op jit(solution)/shard_map/psum | solution.py:96
  874.6 2.4 reduce_sum.36
  (197 shorter events, 66.4 us)
Async XLA Ops:
  7.2 6.5 copy-start
  7.2 9.2 %copy-start.8 = (bf16[256,1024]{1,0:T(8,128)(2,1)S(1)}, bf16[256,1024]{1,0:T(8,128)(2,1)}, u32[]{:S(2)}) copy-start(bf16[256,1024]{1,0:T(8,128)(2,1)} %param.12) | copy-start | bytes 1572868
  7.2 263.5 %all-gather.5.cloned.1.call-start = ((), (), s32[]{:S(2)}) async-start(), calls=%async_computation.2 | async-start | bytes 1064960 | tf_op jit(solution)/shard_map/all_gather | solution.py:21
  7.9 562.4 %all-gather.3.cloned.1.call-start = ((), (), s32[]{:S(2)}) async-start(), calls=%async_computation.1 | async-start | bytes 1064960 | tf_op jit(solution)/shard_map/all_gather | solution.py:20
  577.8 1.5 copy-start.1
  579.3 2.5 copy-start.4
  580.7 2.4 copy-start.2
  580.7 3.4 copy-start.7
  590.9 2.5 copy-start.4
  592.3 2.4 copy-start.2
  592.3 3.4 copy-start.7
  602.5 2.5 copy-start.4
  603.9 2.4 copy-start.2
  603.9 3.4 copy-start.7
  614.1 2.5 copy-start.4
  615.5 2.4 copy-start.2
  615.5 3.4 copy-start.7
  625.7 2.5 copy-start.4
  627.1 2.4 copy-start.2
  627.1 3.4 copy-start.7
  637.3 2.5 copy-start.4
  638.7 2.4 copy-start.2
  638.7 3.4 copy-start.7
  649.0 2.5 copy-start.4
  650.3 2.4 copy-start.2
  650.4 3.4 copy-start.7
  660.6 2.5 copy-start.4
  662.0 2.4 copy-start.2
  662.0 3.4 copy-start.7
  665.3 1.6 copy-start.3
  678.6 194.1 %copy-start.9 = (bf16[8,256,1,128]{3,1,2,0:T(8,128)(2,1)S(1)}, bf16[8,256,1,128]{3,1,2,0:T(8,128)(2,1)}, u32[]{:S(2)}) copy-start(bf16[8,256,1,128]{3,1,2,0:T(8,128)(2,1)} %get-tuple-element.69) | copy-start | bytes 1572868
  678.6 196.0 %all-to-all-start = ((f32[64,64,256]{2,1,0:T(8,128)}), f32[64,64,256]{2,1,0:T(8,128)}, u32[]{:S(2)}, u32[]{:S(2)}) async-start(f32[64,64,256]{2,1,0:T(8,128)} %scatter_fusion), calls=%async_computation | async-start | bytes 8388608 | tf_op jit(solution)/shard_map/all_to_all | solution.py:92
  (23 other events, 29.4 us)
Sparse Core Ops, SparseCore 0:
  10.1 260.5 all-gather.4
  272.8 297.4 all-gather.2
where the time goes:
time: 887 us; the launch traced here: 886 us
  waiting for transfers between devices  552 us (62%)
  blocking collectives  187 us (21%)
  matrix products  61.8 us (7%)
  local copies, waits for them, and re-layouts  30.3 us (3%)
  other arithmetic  24.2 us (3%)
  between operations  16.7 us (2%)
    all_gather x1, waiting for transfers between devices, per_device(): lax.all_gather(image_keys, 'ctx', axis=0, tiled=True)  298 us
    all_gather x1, waiting for transfers between devices, per_device(): lax.all_gather(image_values, 'ctx', axis=0, tiled=True)  253 us
    psum x1, blocking collectives, per_device(): gate_total = lax.psum(gate_acc, ('ctx', 'tp'))  187 us
  transfers between devices with their start and end apart: 3, of which 2 were waited for; matrix products, arithmetic and copies ran while one was open for 1% of the time, Pallas kernels for 0%

commit v1 on v0

--- a/solution.py
+++ b/solution.py
@@ -93,7 +93,7 @@
     summed = jnp.sum(received, axis=0, keepdims=True)
     key_grad = summed[:, :, : local_kv * HD].astype(jnp.bfloat16)
     value_grad = summed[:, :, local_kv * HD :].astype(jnp.bfloat16)
-    gate_total = lax.psum(gate_acc, ("ctx", "tp"))
+    gate_total = lax.psum(lax.psum(gate_acc, "ctx"), "tp")
     term_count = tok_dev * lax.axis_size("ctx") * local_heads * lax.axis_size("tp") * HD
     gate_grad = ((1.0 - gate_value * gate_value) * gate_total / math.sqrt(term_count)).reshape(1)
     return (query_grad, key_grad, value_grad, gate_grad)

time: 887 us -> 955 us (1.077)
  blocking collectives: 187 us -> 255 us
    psum x1 -> x2, blocking collectives: 187 us -> 255 us  [per_device(): gate_total = lax.psum(lax.psum(gate_acc, 'ctx'), 'tp')]
where the time goes in v1:
time: 955 us; the launch traced here: 954 us
  waiting for transfers between devices  552 us (58%)
  blocking collectives  255 us (27%)
  matrix products  61.8 us (6%)
  local copies, waits for them, and re-layouts  30.3 us (3%)
  other arithmetic  24.2 us (3%)
  between operations  16.7 us (2%)
    all_gather x1, waiting for transfers between devices, per_device(): lax.all_gather(image_keys, 'ctx', axis=0, tiled=True)  298 us
    psum x2, blocking collectives, per_device(): gate_total = lax.psum(lax.psum(gate_acc, 'ctx'), 'tp')  255 us
    all_gather x1, waiting for transfers between devices, per_device(): lax.all_gather(image_values, 'ctx', axis=0, tiled=True)  253 us
  transfers between devices with their start and end apart: 3, of which 2 were waited for; matrix products, arithmetic and copies ran while one was open for 1% of the time, Pallas kernels for 0%

profile of v1, /device:TPU:1, one launch (start us, length us, event | category | flops | bytes accessed | tf_op | source)
XLA Modules:
  0.0 953.7 jit_solution(13649404426227503398)
XLA Ops:
  10.9 2.0 top_k.11
  17.4 253.3 %all-gather.5.cloned.1.call-done = bf16[64,64,128]{2,1,0:T(8,128)(2,1)} async-done(((bf16[1,64,128]{2,1,0:T(8,128)(2,1)}), bf16[64,64,128]{2,1,0:T(8,128)(2,1)}) %all-gather.5.cloned.1.call-update) | async-done | bytes 1048592 | tf_op jit(solution)/shard_map/all_gather | solution.py:21
  270.7 1.9 gather_fusion.4
  272.6 297.7 %all-gather.3.cloned.1.call-done = bf16[64,64,128]{2,1,0:T(8,128)(2,1)} async-done(((bf16[1,64,128]{2,1,0:T(8,128)(2,1)}), bf16[64,64,128]{2,1,0:T(8,128)(2,1)}) %all-gather.3.cloned.1.call-update) | async-done | bytes 1048592 | tf_op jit(solution)/shard_map/all_gather | solution.py:20
  570.4 1.9 gather_fusion.3
  572.4 92.9 %while.17 = (s32[]{:T(128)}, f32[2048,1,128]{0,2,1:T(8,128)}, f32[2048,1,128]{0,2,1:T(8,128)}, f32[]{:T(128)}, bf16[8,256,1,128]{3,1,2,0:T(8,128)(2,1)}, /*index...) while((s32[]{:T(128)}, f32[2048,1,128]{0,2,1:T(8,128)}, ...), condition=%wide.region_7.9_spmd.clone, body=%wide.region_2.8_spmd.clone.sunk | while | flops 814710016 | bytes 48644448 | solution.py:77
  575.2 1.9 fusion.68
  577.8 1.4 fusion.69
  586.8 1.9 fusion.68
  589.4 1.4 fusion.69
  590.9 1.4 fusion.71
  598.4 1.9 fusion.68
  601.0 1.4 fusion.69
  602.5 1.4 fusion.71
  610.1 1.9 fusion.68
  612.7 1.4 fusion.69
  621.7 1.9 fusion.68
  624.3 1.4 fusion.69
  633.3 1.9 fusion.68
  635.9 1.4 fusion.69
  644.9 1.9 fusion.68
  647.5 1.4 fusion.69
  656.5 1.9 fusion.68
  659.1 1.4 fusion.69
  665.3 1.6 copy.40
  668.3 1.4 maximum_select_fusion
  669.8 2.5 broadcast_in_dim.68
  672.2 6.4 scatter_fusion
  678.6 7.4 all-to-all-start
  686.0 202.5 %psum.14 = f32[]{:T(128)} all-reduce(f32[]{:T(128)} %get-tuple-element.72), channel_id=1, replica_groups=mesh['ctx'=64,'tp'=8] {'ctx'}, use_global_device_ids=true, to_apply=%region_10.12 | all-reduce | flops 1 | bytes 8 | tf_op jit(solution)/shard_map/psum | solution.py:96
  888.5 52.2 %psum.15 = f32[]{:T(128)} all-reduce(f32[]{:T(128)} %psum.14), channel_id=1, replica_groups=mesh['ctx'=64,'tp'=8] {'tp'}, use_global_device_ids=true, to_apply=%region_11.13 | all-reduce | flops 1 | bytes 8 | tf_op jit(solution)/shard_map/psum | solution.py:96
  942.6 2.4 reduce_sum.36
  (198 shorter events, 67.8 us)
Async XLA Ops:
  7.2 6.5 copy-start
  7.2 9.2 copy-start.8
  7.2 263.5 %all-gather.5.cloned.1.call-start = ((), (), s32[]{:S(2)}) async-start(), calls=%async_computation.2 | async-start | bytes 1064960 | tf_op jit(solution)/shard_map/all_gather | solution.py:21
  7.9 562.4 %all-gather.3.cloned.1.call-start = ((), (), s32[]{:S(2)}) async-start(), calls=%async_computation.1 | async-start | bytes 1064960 | tf_op jit(solution)/shard_map/all_gather | solution.py:20
  577.8 1.5 copy-start.1
  579.3 2.5 copy-start.4
  580.7 2.4 copy-start.2
  580.7 3.4 copy-start.7
  590.9 2.5 copy-start.4
  592.3 2.4 copy-start.2
  592.3 3.4 copy-start.7
  602.5 2.5 copy-start.4
  603.9 2.4 copy-start.2
  603.9 3.4 copy-start.7
  614.1 2.5 copy-start.4
  615.5 2.4 copy-start.2
  615.5 3.4 copy-start.7
  625.7 2.5 copy-start.4
  627.1 2.4 copy-start.2
  627.1 3.4 copy-start.7
  637.3 2.5 copy-start.4
  638.7 2.4 copy-start.2
  638.7 3.4 copy-start.7
  649.0 2.5 copy-start.4
  650.3 2.4 copy-start.2
  650.4 3.4 copy-start.7
  660.6 2.5 copy-start.4
  662.0 2.4 copy-start.2
  662.0 3.4 copy-start.7
  665.3 1.6 copy-start.3
  678.6 262.1 %copy-start.9 = (bf16[8,256,1,128]{3,1,2,0:T(8,128)(2,1)S(1)}, bf16[8,256,1,128]{3,1,2,0:T(8,128)(2,1)}, u32[]{:S(2)}) copy-start(bf16[8,256,1,128]{3,1,2,0:T(8,128)(2,1)} %get-tuple-element.69) | copy-start | bytes 1572868
  678.6 264.0 %all-to-all-start = ((f32[64,64,256]{2,1,0:T(8,128)}), f32[64,64,256]{2,1,0:T(8,128)}, u32[]{:S(2)}, u32[]{:S(2)}) async-start(f32[64,64,256]{2,1,0:T(8,128)} %scatter_fusion), calls=%async_computation | async-start | bytes 8388608 | tf_op jit(solution)/shard_map/all_to_all | solution.py:92
  (23 other events, 29.4 us)
Sparse Core Ops, SparseCore 0:
  10.1 260.5 all-gather.4
  272.8 297.4 all-gather.2
